TPU v7x, 32 devices: a whole 2x2x4 slice. The times are simulated.
32 devices in a mesh: lat: 8 (over y, x, core), lon: 4 (over z).
Axes of the slice: x: 2, y: 2, z: 4, core: 2. Of those that a mesh axis runs over, the one named last changes fastest.
Arguments:
- grid_state: bfloat16 [120, 192, 128], P('lat', 'lon'), may hold values from -6 to 6
- weight_in: bfloat16 [6, 128, 384], replicated, may hold values from -0.5 to 0.5
- bias_in: float32 [6, 384], replicated, may hold values from -4 to 4
- weight_out: bfloat16 [6, 384, 128], replicated, may hold values from -0.3125 to 0.3125
- quad_weights: float32 [120], replicated, may hold values from 0.5 to 2
- diffusion: float32 [128], replicated, may hold values from 0.3 to 30
- legendre: bfloat16 [32, 120, 32], P('lon'), may hold values from -0.5 to 0.5
- chan_table: int32 [128], replicated, may hold values from 0 to 127, each once
- wave_table: int32 [32], replicated, may hold values from 0 to 31, each once
Outputs:
- updated: bfloat16 [120, 192, 128], P('lat', 'lon')
- spectral: float32 [32, 128, 2, 32], P('lon', 'lat')
Inputs may be any that keep to these rules, and one draw needn't show every extreme that they name: `chan_table`: each channel 0 to 127 stands exactly once. `wave_table`: each wavenumber 0 to 31 stands exactly once.
All inputs are finite; a program needn't handle non-finite values.
Results may differ from a plain program's by a relative error of at most 0.012.
Values may be sent and summed in bfloat16 or wider, within the bound.
A program may use at most 64 MiB of HBM per device.

v0:
```python
import math

import jax
import jax.numpy as jnp
from jax import lax
from jax.sharding import PartitionSpec as P


def column_layers(column_rows, weight_in, bias_in, weight_out):
    hidden_state = column_rows.astype(jnp.float32)
    for layer_idx in range(weight_in.shape[0]):
        inv_rms = lax.rsqrt(jnp.mean(hidden_state * hidden_state, axis=-1, keepdims=True) + 1e-06)
        normed = (hidden_state * inv_rms).astype(jnp.bfloat16)
        pre_act = (
            jnp.dot(normed, weight_in[layer_idx], preferred_element_type=jnp.float32)
            + bias_in[layer_idx]
        )
        activation = jax.nn.gelu(pre_act, approximate=True).astype(jnp.bfloat16)
        hidden_state = hidden_state + jnp.dot(
            activation, weight_out[layer_idx], preferred_element_type=jnp.float32
        )
    return hidden_state.astype(jnp.bfloat16)


def trig_table(wave_ids, longitudes, lon_total):
    phase_angle = (wave_ids[:, None] * longitudes[None, :] % lon_total).astype(jnp.float32) * (
        2.0 * math.pi / lon_total
    )
    stacked = jnp.stack([jnp.cos(phase_angle), -jnp.sin(phase_angle)], axis=1) / math.sqrt(
        lon_total
    )
    return stacked.astype(jnp.bfloat16)


def local(
    grid_state,
    weight_in,
    bias_in,
    weight_out,
    quad_weights,
    diffusion,
    legendre,
    chan_table,
    wave_table,
):
    lat_rows, lon_cols, channels = grid_state.shape
    lat_count = lax.axis_size("lat")
    lon_count = lax.axis_size("lon")
    lon_total = lon_cols * lon_count
    per_dev = channels // lat_count
    owned_slots = legendre.shape[0]
    top_degree = legendre.shape[2]
    flat_rows = grid_state.reshape(lat_rows * lon_cols, channels)
    columns = column_layers(flat_rows, weight_in, bias_in, weight_out).reshape(
        lat_rows, lon_cols, channels
    )
    ordered = jnp.take(columns, chan_table, axis=2)
    levels = lax.all_to_all(ordered, "lat", split_axis=2, concat_axis=0, tiled=True)
    trig_all = trig_table(wave_table, jnp.arange(lon_total, dtype=jnp.int32), lon_total)
    lon_here = lax.axis_index("lon") * lon_cols + jnp.arange(lon_cols, dtype=jnp.int32)
    trig_rows = trig_table(wave_table, lon_here, lon_total)
    fourier = lax.psum_scatter(
        jnp.einsum("srj,ljk->skrl", trig_rows, levels, preferred_element_type=jnp.float32),
        "lon",
        scatter_dimension=0,
        tiled=True,
    )
    weighted = (fourier * quad_weights).astype(jnp.bfloat16)
    raw_spec = jnp.einsum("skrl,sln->skrn", weighted, legendre, preferred_element_type=jnp.float32)
    my_waves = lax.dynamic_slice_in_dim(
        wave_table, lax.axis_index("lon") * owned_slots, owned_slots, 0
    )
    degree = jnp.arange(top_degree, dtype=jnp.int32)
    triangle = (degree[None, :] >= my_waves[:, None]).astype(jnp.float32)
    my_chans = lax.dynamic_slice_in_dim(chan_table, lax.axis_index("lat") * per_dev, per_dev, 0)
    degree_f = degree.astype(jnp.float32)
    damping = (
        jnp.take(diffusion, my_chans)[:, None]
        * (degree_f * (degree_f + 1.0))[None, :]
        / float(top_degree * top_degree)
    )
    spectral = raw_spec * triangle[:, None, None, :] / (1.0 + damping)[None, :, None, :]
    back_fourier = jnp.einsum(
        "skrn,sln->skrl",
        spectral.astype(jnp.bfloat16),
        legendre,
        preferred_element_type=jnp.float32,
    ).astype(jnp.bfloat16)
    all_waves = lax.all_to_all(back_fourier, "lon", split_axis=3, concat_axis=0, tiled=True)
    band_tendency = jnp.einsum(
        "skrl,srj->ljk", all_waves, trig_all, preferred_element_type=jnp.float32
    ).astype(jnp.bfloat16)
    tendency = lax.all_to_all(
        lax.all_to_all(band_tendency, "lon", split_axis=1, concat_axis=0, tiled=True),
        "lat",
        split_axis=0,
        concat_axis=2,
        tiled=True,
    )
    tendency = jnp.take(tendency, jnp.argsort(chan_table), axis=2)
    updated = (columns.astype(jnp.float32) + tendency.astype(jnp.float32)).astype(jnp.bfloat16)
    return (updated, spectral)


def solution(mesh):
    placed = (P("lat", "lon", None), P(), P(), P(), P(), P(), P("lon", None, None), P(), P())
    return jax.shard_map(
        local,
        mesh=mesh,
        in_specs=placed,
        out_specs=(P("lat", "lon", None), P("lon", "lat", None, None)),
        check_vma=False,
    )
```

profile of v0, /device:TPU:0, one launch (start us, length us, event | category | flops | bytes accessed | tf_op | source)
XLA Modules:
  0.0 105.2 jit_solution(2320604026377320569)
XLA Ops:
  7.2 0.7 compare_select_fusion.1
  7.9 0.7 compare_and_fusion.1
  8.5 1.0 slice_reduce_fusion
  9.5 1.1 %multiply_reduce_fusion.5 = f32[15,48]{1,0:T(8,128)S(1)} fusion(bf16[15,48,128]{2,1,0:T(8,128)(2,1)} %param.11), kind=kLoop, calls=%fused_computation.121 | loop fusion | flops 275760 | bytes 187200 | tf_op jit(solution)/shard_map/reduce_sum | solution.py:12
  10.6 1.1 %multiply_convert_fusion.15 = bf16[15,48,128]{2,1,0:T(8,128)(2,1)S(1)} fusion(bf16[15,48,128]{2,1,0:T(8,128)(2,1)} %param.11, f32[15,48]{1,0:T(8,128)S(1)} %add_rsqrt_fusion), kind=kLoop, calls=%fused_computation.120 | loop fusion | flops 276480 | bytes 371520 | tf_op jit(solution)/shard_map/convert_element_type | solution.py:13
  11.7 1.9 %multiply_reduce_fusion.4 = (f32[720]{0:T(1024)S(1)}, f32[720,128]{1,0:T(8,128)S(1)}) fusion(bf16[6,384,128]{2,1,0:T(8,128)(2,1)} %param.14, bf16[720,128]{1,0:T(8,128)(2,1)S(1)} %bitcast.137, f32[384]{0:T(512)S(1)} %get-tuple-element.15, bf16[6,128,384]{2,1,0:T(8,128)(2,1)} %param.12, bf16[720,128]{1,0:T(8,128)(2,1)} %bitcast.136), kind=kOutput, calls=%fused_computation.119 | convolution fusion | flops 144690480 | bytes 938304 | tf_op jit(solution)/shard_map/dot_general | solution.py:19
  13.7 0.9 multiply_reduce_fusion.3
  14.6 0.9 multiply_reduce_fusion.2
  15.4 0.9 multiply_reduce_fusion.1
  16.3 0.9 multiply_reduce_fusion
  17.2 0.8 fusion.1
  18.0 0.4 copy.25
  18.5 0.7 gather_fusion.1
  19.2 0.2 fusion.193
  19.4 1.4 %reshape.364 = bf16[8,2,5760]{2,1,0:T(2,128)(2,1)} reshape(bf16[128,15,48]{2,1,0:T(8,128)(2,1)S(1)} %fusion.193) | data formatting | bytes 368640
  20.8 5.2 %all-to-all-start = ((bf16[8,2,5760]{2,1,0:T(2,128)(2,1)}), bf16[8,2,5760]{2,1,0:T(2,128)(2,1)S(1)}, u32[]{:S(2)}, u32[]{:S(2)}) async-start(bf16[8,2,5760]{2,1,0:T(2,128)(2,1)} %reshape.364), calls=%async_computation | async-start | bytes 368640 | tf_op jit(solution)/shard_map/all_to_all | solution.py:58
  26.1 0.2 fusion.152
  26.3 5.8 %all-to-all-done = bf16[8,2,5760]{2,1,0:T(2,128)(2,1)S(1)} async-done(((bf16[8,2,5760]{2,1,0:T(2,128)(2,1)}), bf16[8,2,5760]{2,1,0:T(2,128)(2,1)S(1)}, u32[]{:S(2)}, u32[]{:S(2)}) %all-to-all-start) | async-done | bytes 184352 | tf_op jit(solution)/shard_map/all_to_all | solution.py:58
  32.0 0.6 reshape.365
  32.8 1.2 %convolution_bitcast_fusion.1 = f32[32,16,2,120]{3,0,2,1:T(8,128)} fusion(bf16[120,48,16,1]{1,2,0,3:T(8,128)(2,1)S(1)} %bitcast.129, f32[32,1,48]{2,0,1:T(8,128)S(1)} %get-tuple-element.18, f32[32,1,48]{2,0,1:T(8,128)S(1)} %get-tuple-element.17), kind=kOutput, calls=%fused_computation.16 | convolution fusion | flops 11805696 | bytes 688128 | tf_op jit(solution)/shard_map/srj,ljk->skrl/dot_general | solution.py:63
  34.2 0.7 gather_fusion
  35.1 20.2 %reduce-scatter.2.cloned.1.call-done = f32[8,16,2,120]{3,0,2,1:T(8,128)} async-done(((f32[32,16,2,120]{3,0,2,1:T(8,128)}), f32[8,16,2,120]{3,0,2,1:T(8,128)}) %reduce-scatter.2.cloned.1.call-update) | async-done | bytes 122896 | tf_op jit(solution)/shard_map/reduce_scatter | solution.py:62
  55.2 0.9 multiply_convert_fusion.16
  56.2 0.2 fusion.3
  56.5 0.5 copy.31
  56.9 1.0 reshape.366
  58.0 3.3 %all-to-all-start.1 = ((bf16[4,2,3840]{2,1,0:T(2,128)(2,1)}), bf16[4,2,3840]{2,1,0:T(2,128)(2,1)S(1)}, u32[]{:S(2)}, u32[]{:S(2)}) async-start(bf16[4,2,3840]{2,1,0:T(2,128)(2,1)} %reshape.366), calls=%async_computation.2 | async-start | bytes 122880 | tf_op jit(solution)/shard_map/all_to_all | solution.py:89
  61.3 0.2 fusion.143
  61.5 5.5 %all-to-all-done.1 = bf16[4,2,3840]{2,1,0:T(2,128)(2,1)S(1)} async-done(((bf16[4,2,3840]{2,1,0:T(2,128)(2,1)}), bf16[4,2,3840]{2,1,0:T(2,128)(2,1)S(1)}, u32[]{:S(2)}, u32[]{:S(2)}) %all-to-all-start.1) | async-done | bytes 61472 | tf_op jit(solution)/shard_map/all_to_all | solution.py:89
  67.0 0.4 reshape.367
  67.3 0.9 copy.48
  68.2 0.3 fusion.2
  68.5 0.7 copy.34
  69.2 2.1 %reshape.368 = bf16[4,2,11520]{2,1,0:T(2,128)(2,1)} reshape(bf16[192,16,30]{2,1,0:T(8,128)(2,1)S(1)} %bitcast.127) | data formatting | bytes 368640
  71.3 3.5 %all-to-all-start.2 = ((bf16[4,2,11520]{2,1,0:T(2,128)(2,1)}), bf16[4,2,11520]{2,1,0:T(2,128)(2,1)S(1)}, u32[]{:S(2)}, u32[]{:S(2)}) async-start(bf16[4,2,11520]{2,1,0:T(2,128)(2,1)} %reshape.368), calls=%async_computation.3 | async-start | bytes 368640 | tf_op jit(solution)/shard_map/all_to_all | solution.py:94
  74.9 2.5 %sort.17 = (s32[128]{0:T(128)}, s32[128]{0:T(128)S(1)}) sort(s32[128]{0:T(128)S(1)} %copy-done.4, s32[128]{0:T(128)S(1)} %iota.31), dimensions={0}, to_apply=%region_7.9 | sort | flops 896 | bytes 2048 | tf_op jit(solution)/shard_map/jit(argsort)/sort | solution.py:100
  77.4 3.4 %all-to-all-done.2 = bf16[4,2,11520]{2,1,0:T(2,128)(2,1)S(1)} async-done(((bf16[4,2,11520]{2,1,0:T(2,128)(2,1)}), bf16[4,2,11520]{2,1,0:T(2,128)(2,1)S(1)}, u32[]{:S(2)}, u32[]{:S(2)}) %all-to-all-start.2) | async-done | bytes 184352 | tf_op jit(solution)/shard_map/all_to_all | solution.py:94
  80.8 2.1 %reshape.369 = bf16[192,16,30]{2,1,0:T(8,128)(2,1)S(1)} reshape(bf16[4,2,11520]{2,1,0:T(2,128)(2,1)S(1)} %all-to-all-done.2) | data formatting | bytes 368640
  82.9 1.3 %copy.47 = bf16[30,4,48,16]{2,1,3,0:T(4,128)(2,1)S(1)} copy(bf16[30,4,48,16]{0,3,2,1:T(8,128)(2,1)S(1)} %bitcast.126) | data formatting | bytes 368640 | tf_op jit(solution)/shard_map/all_to_all | solution.py:94
  84.3 1.4 %reshape.370 = bf16[8,2,5760]{2,1,0:T(2,128)(2,1)} reshape(bf16[120,16,48]{2,1,0:T(8,128)(2,1)S(1)} %bitcast.133) | data formatting | bytes 368640
  85.7 3.6 %all-to-all-start.3 = ((bf16[8,2,5760]{2,1,0:T(2,128)(2,1)}), bf16[8,2,5760]{2,1,0:T(2,128)(2,1)S(1)}, u32[]{:S(2)}, u32[]{:S(2)}) async-start(bf16[8,2,5760]{2,1,0:T(2,128)(2,1)} %reshape.370), calls=%async_computation.4 | async-start | bytes 368640 | tf_op jit(solution)/shard_map/all_to_all | solution.py:93
  89.3 0.7 copy.40
  90.0 5.4 %all-to-all-done.3 = bf16[8,2,5760]{2,1,0:T(2,128)(2,1)S(1)} async-done(((bf16[8,2,5760]{2,1,0:T(2,128)(2,1)}), bf16[8,2,5760]{2,1,0:T(2,128)(2,1)S(1)}, u32[]{:S(2)}, u32[]{:S(2)}) %all-to-all-start.3) | async-done | bytes 184352 | tf_op jit(solution)/shard_map/all_to_all | solution.py:93
  95.4 0.5 reshape.371
  95.9 0.3 copy.38
  96.3 0.7 gather_fusion.2
  97.0 0.3 add_convert_fusion
  97.3 1.1 %copy.39 = bf16[15,48,128]{2,1,0:T(8,128)(2,1)} copy(bf16[15,48,128]{1,0,2:T(8,128)(2,1)S(1)} %add_convert_fusion) | data formatting | bytes 368640
  (39 shorter events, 1.0 us)
Async XLA Ops:
  7.2 49.0 %copy-start = (bf16[8,120,32]{1,2,0:T(8,128)(2,1)S(1)}, bf16[8,120,32]{1,2,0:T(8,128)(2,1)}, u32[]{:S(2)}) copy-start(bf16[8,120,32]{1,2,0:T(8,128)(2,1)} %param.17) | copy-start | bytes 184324
  11.7 1.9 %copy-start.5 = (bf16[6,384,128]{2,1,0:T(8,128)(2,1)S(1)}, bf16[6,384,128]{2,1,0:T(8,128)(2,1)}, u32[]{:S(2)}) copy-start(bf16[6,384,128]{2,1,0:T(8,128)(2,1)} %param.14) | copy-start | bytes 1769476
  11.7 1.9 %copy-start.6 = (bf16[6,128,384]{2,1,0:T(8,128)(2,1)S(1)}, bf16[6,128,384]{2,1,0:T(8,128)(2,1)}, u32[]{:S(2)}) copy-start(bf16[6,128,384]{2,1,0:T(8,128)(2,1)} %param.12) | copy-start | bytes 1769476
  19.4 6.6 %copy-start.2 = (s32[32]{0:T(128)S(1)}, s32[32]{0:T(128)}, u32[]{:S(2)}) copy-start(s32[32]{0:T(128)} %param.19) | copy-start | bytes 388
  20.8 11.3 %all-to-all-start = ((bf16[8,2,5760]{2,1,0:T(2,128)(2,1)}), bf16[8,2,5760]{2,1,0:T(2,128)(2,1)S(1)}, u32[]{:S(2)}, u32[]{:S(2)}) async-start(bf16[8,2,5760]{2,1,0:T(2,128)(2,1)} %reshape.364), calls=%async_computation | async-start | bytes 368640 | tf_op jit(solution)/shard_map/all_to_all | solution.py:58
  25.9 29.3 %reduce-scatter.2.cloned.1.call-start = ((), (), s32[]{:S(2)}) async-start(), calls=%async_computation.5 | async-start | bytes 655360 | tf_op jit(solution)/shard_map/reduce_scatter | solution.py:62
  32.8 1.3 %copy-start.4 = (s32[128]{0:T(128)S(1)}, s32[128]{0:T(128)}, u32[]{:S(2)}) copy-start(s32[128]{0:T(128)} %param.18) | copy-start | bytes 1540
  32.8 1.4 %copy-start.1 = (f32[128]{0:T(128)S(1)}, f32[128]{0:T(128)}, u32[]{:S(2)}) copy-start(f32[128]{0:T(128)} %param.16) | copy-start | bytes 1540
  34.0 21.2 %copy-start.3 = (f32[120]{0:T(128)S(1)}, f32[120]{0:T(128)}, u32[]{:S(2)}) copy-start(f32[120]{0:T(128)} %param.15) | copy-start | bytes 1444
  58.0 9.0 %all-to-all-start.1 = ((bf16[4,2,3840]{2,1,0:T(2,128)(2,1)}), bf16[4,2,3840]{2,1,0:T(2,128)(2,1)S(1)}, u32[]{:S(2)}, u32[]{:S(2)}) async-start(bf16[4,2,3840]{2,1,0:T(2,128)(2,1)} %reshape.366), calls=%async_computation.2 | async-start | bytes 122880 | tf_op jit(solution)/shard_map/all_to_all | solution.py:89
  71.3 9.5 %all-to-all-start.2 = ((bf16[4,2,11520]{2,1,0:T(2,128)(2,1)}), bf16[4,2,11520]{2,1,0:T(2,128)(2,1)S(1)}, u32[]{:S(2)}, u32[]{:S(2)}) async-start(bf16[4,2,11520]{2,1,0:T(2,128)(2,1)} %reshape.368), calls=%async_computation.3 | async-start | bytes 368640 | tf_op jit(solution)/shard_map/all_to_all | solution.py:94
  85.7 9.7 %all-to-all-start.3 = ((bf16[8,2,5760]{2,1,0:T(2,128)(2,1)}), bf16[8,2,5760]{2,1,0:T(2,128)(2,1)S(1)}, u32[]{:S(2)}, u32[]{:S(2)}) async-start(bf16[8,2,5760]{2,1,0:T(2,128)(2,1)} %reshape.370), calls=%async_computation.4 | async-start | bytes 368640 | tf_op jit(solution)/shard_map/all_to_all | solution.py:93
Sparse Core Ops, SparseCore 0:
  34.2 20.9 reduce-scatter.1
where the time goes:
time: 106 us; the launch traced here: 105 us
  waiting for transfers between devices  40.2 us (38%)
  local copies, waits for them, and re-layouts  18.8 us (18%)
  starting transfers between devices  15.6 us (15%)
  between operations  14.4 us (14%)
  other arithmetic  8.25 us (8%)
  matrix products  8.03 us (8%)
    reduce_scatter x1, waiting for transfers between devices, local(): lax.psum_scatter(jnp.einsum('srj,ljk->skrl', trig_rows, levels, preferred...  20.2 us
    unnamed x24, local copies, waits for them, and re-layouts  11.4 us
    dot_general x6, matrix products, column_layers(): jnp.dot(activation, weight_out[layer_idx], preferred_element_type=jnp.flo...  6.23 us
    all_to_all x1, waiting for transfers between devices, local(): lax.all_to_all(ordered, 'lat', split_axis=2, concat_axis=0, tiled=True)  5.79 us
    all_to_all x1, waiting for transfers between devices, local(): lax.all_to_all(back_fourier, 'lon', split_axis=3, concat_axis=0, tiled=True)  5.47 us
    all_to_all x1, waiting for transfers between devices, local(): lax.all_to_all(lax.all_to_all(band_tendency, 'lon', split_axis=1, concat_...  5.36 us
    all_to_all x1, starting transfers between devices, local(): lax.all_to_all(ordered, 'lat', split_axis=2, concat_axis=0, tiled=True)  5.16 us
    all_to_all x1, starting transfers between devices, local(): lax.all_to_all(lax.all_to_all(band_tendency, 'lon', split_axis=1, concat_...  3.6 us
  transfers between devices with their start and end apart: 5, of which 5 were waited for; matrix products, arithmetic and copies ran while one was open for 4% of the time, Pallas kernels for 0%

commit v1 on v0

--- a/solution.py
+++ b/solution.py
@@ -32,6 +32,11 @@
     return stacked.astype(jnp.bfloat16)
 
 
+def pick_channels(rows, chosen):
+    picked = jnp.einsum("ljc,ck->ljk", rows, chosen, preferred_element_type=jnp.float32)
+    return picked.astype(jnp.bfloat16)
+
+
 def local(
     grid_state,
     weight_in,
@@ -54,7 +59,9 @@
     columns = column_layers(flat_rows, weight_in, bias_in, weight_out).reshape(
         lat_rows, lon_cols, channels
     )
-    ordered = jnp.take(columns, chan_table, axis=2)
+    every = jnp.arange(channels, dtype=jnp.int32)
+    chosen = (every[:, None] == chan_table[None, :]).astype(jnp.bfloat16)
+    ordered = pick_channels(columns, chosen)
     levels = lax.all_to_all(ordered, "lat", split_axis=2, concat_axis=0, tiled=True)
     trig_all = trig_table(wave_table, jnp.arange(lon_total, dtype=jnp.int32), lon_total)
     lon_here = lax.axis_index("lon") * lon_cols + jnp.arange(lon_cols, dtype=jnp.int32)
@@ -75,7 +82,7 @@
     my_chans = lax.dynamic_slice_in_dim(chan_table, lax.axis_index("lat") * per_dev, per_dev, 0)
     degree_f = degree.astype(jnp.float32)
     damping = (
-        jnp.take(diffusion, my_chans)[:, None]
+        jnp.sum(jnp.where(my_chans[:, None] == every[None, :], diffusion[None, :], 0.0), 1)[:, None]
         * (degree_f * (degree_f + 1.0))[None, :]
         / float(top_degree * top_degree)
     )
@@ -97,7 +104,7 @@
         concat_axis=2,
         tiled=True,
     )
-    tendency = jnp.take(tendency, jnp.argsort(chan_table), axis=2)
+    tendency = pick_channels(tendency, chosen.T)
     updated = (columns.astype(jnp.float32) + tendency.astype(jnp.float32)).astype(jnp.bfloat16)
     return (updated, spectral)
 

time: 106 us -> 101 us (0.953)
  blocking collectives: 0 us -> 9.13 us
  other arithmetic: 8.25 us -> 3.88 us
  local copies, waits for them, and re-layouts: 18.8 us -> 14.7 us
  starting transfers between devices: 15.6 us -> 12.1 us
  waiting for transfers between devices: 40.2 us -> 37.4 us
  matrix products: 8.03 us -> 9.23 us
    all_to_all x0 -> x1, blocking collectives: none -> 9.13 us  [local(): lax.all_to_all(band_tendency, 'lon', split_axis=1, concat_axis=0, tiled=T...]
    all_to_all x1 -> x0, starting transfers between devices: 3.54 us -> none  [local(): lax.all_to_all(band_tendency, 'lon', split_axis=1, concat_axis=0, tiled=T...]
    all_to_all x1 -> x0, waiting for transfers between devices: 3.39 us -> none  [local(): lax.all_to_all(band_tendency, 'lon', split_axis=1, concat_axis=0, tiled=T...]
    sort x1 -> x0, other arithmetic: 2.54 us -> none  [local(): tendency = jnp.take(tendency, jnp.argsort(chan_table), axis=2)]
    gather x3 -> x0, local copies, waits for them, and re-layouts: 2.07 us -> none  [the longest x1 0.71 us: local(): tendency = jnp.take(tendency, jnp.argsort(chan_table), axis=2)]
    unnamed x24 -> x23, local copies, waits for them, and re-layouts: 11.4 us -> 9.62 us
    dot_general x0 -> x2, matrix products: none -> 1.21 us  [pick_channels(): jnp.einsum('ljc,ck->ljk', rows, chosen, preferred_element_type=jnp.float32)]
  transfers between devices with their start and end apart: 5 -> 4, of which waited for: 5 -> 4; matrix products, arithmetic and copies ran while one was open for 4% -> 2% of each run, Pallas kernels for 0% -> 0%
where the time goes in v1:
time: 101 us
  waiting for transfers between devices  37.4 us (37%)
  local copies, waits for them, and re-layouts  14.7 us (15%)
  between operations  14.3 us (14%)
  starting transfers between devices  12.1 us (12%)
  matrix products  9.23 us (9%)
  blocking collectives  9.13 us (9%)
  other arithmetic  3.88 us (4%)
    reduce_scatter x1, waiting for transfers between devices, local(): lax.psum_scatter(jnp.einsum('srj,ljk->skrl', trig_rows, levels, preferred...  20.7 us
    unnamed x23, local copies, waits for them, and re-layouts  9.62 us
    all_to_all x1, blocking collectives, local(): lax.all_to_all(band_tendency, 'lon', split_axis=1, concat_axis=0, tiled=T...  9.13 us
    dot_general x6, matrix products, column_layers(): jnp.dot(activation, weight_out[layer_idx], preferred_element_type=jnp.flo...  6.23 us
    all_to_all x1, waiting for transfers between devices, local(): lax.all_to_all(ordered, 'lat', split_axis=2, concat_axis=0, tiled=True)  5.87 us
    all_to_all x1, waiting for transfers between devices, local(): lax.all_to_all(back_fourier, 'lon', split_axis=3, concat_axis=0, tiled=True)  5.47 us
    all_to_all x1, waiting for transfers between devices, local(): lax.all_to_all(lax.all_to_all(band_tendency, 'lon', split_axis=1, concat_...  5.38 us
    all_to_all x1, starting transfers between devices, local(): lax.all_to_all(ordered, 'lat', split_axis=2, concat_axis=0, tiled=True)  5.18 us
  transfers between devices with their start and end apart: 4, of which 4 were waited for; matrix products, arithmetic and copies ran while one was open for 2% of the time, Pallas kernels for 0%

profile of v1, /device:TPU:0, one launch (start us, length us, event | category | flops | bytes accessed | tf_op | source)
XLA Modules:
  0.0 100.8 jit_solution(6014327949595269104)
XLA Ops:
  7.2 1.1 %multiply_reduce_fusion.5 = f32[15,48]{1,0:T(8,128)S(1)} fusion(bf16[15,48,128]{2,1,0:T(8,128)(2,1)} %param.9), kind=kLoop, calls=%fused_computation.121 | loop fusion | flops 275760 | bytes 187200 | tf_op jit(solution)/shard_map/reduce_sum | solution.py:12
  8.3 1.0 slice_reduce_fusion
  9.3 1.1 %multiply_convert_fusion.15 = bf16[15,48,128]{2,1,0:T(8,128)(2,1)S(1)} fusion(bf16[15,48,128]{2,1,0:T(8,128)(2,1)} %param.9, f32[15,48]{1,0:T(8,128)S(1)} %add_rsqrt_fusion), kind=kLoop, calls=%fused_computation.120 | loop fusion | flops 276480 | bytes 371520 | tf_op jit(solution)/shard_map/convert_element_type | solution.py:13
  10.4 1.9 %multiply_reduce_fusion.4 = (f32[720]{0:T(1024)S(1)}, f32[720,128]{1,0:T(8,128)S(1)}) fusion(bf16[6,384,128]{2,1,0:T(8,128)(2,1)} %param.12, bf16[720,128]{1,0:T(8,128)(2,1)S(1)} %bitcast.139, f32[384]{0:T(512)S(1)} %get-tuple-element.14, bf16[6,128,384]{2,1,0:T(8,128)(2,1)} %param.10, bf16[720,128]{1,0:T(8,128)(2,1)} %bitcast.136), kind=kOutput, calls=%fused_computation.119 | convolution fusion | flops 144690480 | bytes 938304 | tf_op jit(solution)/shard_map/dot_general | solution.py:19
  12.3 0.9 multiply_reduce_fusion.3
  13.2 0.9 multiply_reduce_fusion.2
  14.1 0.9 multiply_reduce_fusion.1
  15.0 0.9 multiply_reduce_fusion
  15.9 0.8 fusion.4
  16.7 0.2 convolution_convert_fusion.1
  17.0 0.4 copy.36
  17.4 1.4 %reshape.324 = bf16[8,2,5760]{2,1,0:T(2,128)(2,1)} reshape(bf16[128,15,48]{2,1,0:T(8,128)(2,1)S(1)} %bitcast.127) | data formatting | bytes 368640
  18.8 5.2 %all-to-all-start = ((bf16[8,2,5760]{2,1,0:T(2,128)(2,1)}), bf16[8,2,5760]{2,1,0:T(2,128)(2,1)S(1)}, u32[]{:S(2)}, u32[]{:S(2)}) async-start(bf16[8,2,5760]{2,1,0:T(2,128)(2,1)} %reshape.324), calls=%async_computation | async-start | bytes 368640 | tf_op jit(solution)/shard_map/all_to_all | solution.py:65
  24.0 0.0 reduce-scatter.2.cloned.1.call-start
  24.0 0.2 fusion.160
  24.2 5.9 %all-to-all-done = bf16[8,2,5760]{2,1,0:T(2,128)(2,1)S(1)} async-done(((bf16[8,2,5760]{2,1,0:T(2,128)(2,1)}), bf16[8,2,5760]{2,1,0:T(2,128)(2,1)S(1)}, u32[]{:S(2)}, u32[]{:S(2)}) %all-to-all-start) | async-done | bytes 184352 | tf_op jit(solution)/shard_map/all_to_all | solution.py:65
  30.1 0.6 reshape.325
  30.7 0.1 copy.38
  30.8 1.2 %convolution_bitcast_fusion.1 = f32[32,16,2,120]{3,0,2,1:T(8,128)} fusion(bf16[120,48,16,1]{1,2,0,3:T(8,128)(2,1)S(1)} %bitcast.129, f32[32,1,48]{2,0,1:T(8,128)S(1)} %get-tuple-element.17, f32[32,1,48]{2,0,1:T(8,128)S(1)} %get-tuple-element.16), kind=kOutput, calls=%fused_computation.13 | convolution fusion | flops 11805696 | bytes 688128 | tf_op jit(solution)/shard_map/srj,ljk->skrl/dot_general | solution.py:70
  32.1 0.1 dynamic_slice.7
  32.2 0.1 dynamic_slice.6
  32.3 0.2 select_reduce_fusion
  32.4 0.1 fusion.162
  32.5 0.1 multiply_add_fusion
  32.6 20.7 %reduce-scatter.2.cloned.1.call-done = f32[8,16,2,120]{3,0,2,1:T(8,128)} async-done(((f32[32,16,2,120]{3,0,2,1:T(8,128)}), f32[8,16,2,120]{3,0,2,1:T(8,128)}) %reduce-scatter.2.cloned.1.call-update) | async-done | bytes 122896 | tf_op jit(solution)/shard_map/reduce_scatter | solution.py:69
  53.3 0.9 multiply_convert_fusion.16
  54.2 0.2 fusion.6
  54.4 0.1 convolution_convert_fusion.2
  54.5 0.5 copy.41
  55.0 1.0 %reshape.326 = bf16[4,2,3840]{2,1,0:T(2,128)(2,1)} reshape(bf16[120,8,2,16]{3,2,1,0:T(2,128)(2,1)S(1)} %bitcast.131) | data formatting | bytes 122880
  56.0 3.3 %all-to-all-start.1 = ((bf16[4,2,3840]{2,1,0:T(2,128)(2,1)}), bf16[4,2,3840]{2,1,0:T(2,128)(2,1)S(1)}, u32[]{:S(2)}, u32[]{:S(2)}) async-start(bf16[4,2,3840]{2,1,0:T(2,128)(2,1)} %reshape.326), calls=%async_computation.2 | async-start | bytes 122880 | tf_op jit(solution)/shard_map/all_to_all | solution.py:96
  59.3 0.2 fusion.151
  59.5 5.5 %all-to-all-done.1 = bf16[4,2,3840]{2,1,0:T(2,128)(2,1)S(1)} async-done(((bf16[4,2,3840]{2,1,0:T(2,128)(2,1)}), bf16[4,2,3840]{2,1,0:T(2,128)(2,1)S(1)}, u32[]{:S(2)}, u32[]{:S(2)}) %all-to-all-start.1) | async-done | bytes 61472 | tf_op jit(solution)/shard_map/all_to_all | solution.py:96
  65.0 0.4 reshape.327
  65.4 0.9 copy.58
  66.3 0.3 fusion.5
  66.5 0.7 copy.44
  67.2 1.4 %reshape.328 = bf16[4,2,11520]{2,1,0:T(2,128)(2,1)S(1)} reshape(bf16[192,16,30]{2,1,0:T(8,128)(2,1)S(1)} %bitcast.126) | data formatting | bytes 368640
  68.7 9.1 %all_to_all.72 = bf16[4,2,11520]{2,1,0:T(2,128)(2,1)S(1)} all-to-all(bf16[4,2,11520]{2,1,0:T(2,128)(2,1)S(1)} %reshape.328), channel_id=1, replica_groups=mesh['lat'=8,'lon'=4] {'lon'}, dimensions={0} | all-to-all | bytes 368640 | tf_op jit(solution)/shard_map/all_to_all | solution.py:101
  77.8 2.1 %reshape.329 = bf16[192,16,30]{2,1,0:T(8,128)(2,1)S(1)} reshape(bf16[4,2,11520]{2,1,0:T(2,128)(2,1)S(1)} %all_to_all.72) | data formatting | bytes 368640
  79.9 1.3 %copy.57 = bf16[30,4,48,16]{2,1,3,0:T(4,128)(2,1)S(1)} copy(bf16[30,4,48,16]{0,3,2,1:T(8,128)(2,1)S(1)} %bitcast.125) | data formatting | bytes 368640 | tf_op jit(solution)/shard_map/all_to_all | solution.py:101
  81.3 0.1 copy.46
  81.3 1.4 %reshape.330 = bf16[8,2,5760]{2,1,0:T(2,128)(2,1)} reshape(bf16[120,16,48]{2,1,0:T(8,128)(2,1)S(1)} %bitcast.134) | data formatting | bytes 368640
  82.7 3.6 %all-to-all-start.3 = ((bf16[8,2,5760]{2,1,0:T(2,128)(2,1)}), bf16[8,2,5760]{2,1,0:T(2,128)(2,1)S(1)}, u32[]{:S(2)}, u32[]{:S(2)}) async-start(bf16[8,2,5760]{2,1,0:T(2,128)(2,1)} %reshape.330), calls=%async_computation.4 | async-start | bytes 368640 | tf_op jit(solution)/shard_map/all_to_all | solution.py:100
  86.3 0.7 copy.49
  87.0 5.4 %all-to-all-done.3 = bf16[8,2,5760]{2,1,0:T(2,128)(2,1)S(1)} async-done(((bf16[8,2,5760]{2,1,0:T(2,128)(2,1)}), bf16[8,2,5760]{2,1,0:T(2,128)(2,1)S(1)}, u32[]{:S(2)}, u32[]{:S(2)}) %all-to-all-start.3) | async-done | bytes 184352 | tf_op jit(solution)/shard_map/all_to_all | solution.py:100
  92.4 0.5 reshape.331
  92.9 1.0 fusion.3
  (24 shorter events, 0.2 us)
Async XLA Ops:
  7.2 47.0 %copy-start = (bf16[8,120,32]{1,2,0:T(8,128)(2,1)S(1)}, bf16[8,120,32]{1,2,0:T(8,128)(2,1)}, u32[]{:S(2)}) copy-start(bf16[8,120,32]{1,2,0:T(8,128)(2,1)} %param.15) | copy-start | bytes 184324
  10.4 1.9 %copy-start.4 = (bf16[6,384,128]{2,1,0:T(8,128)(2,1)S(1)}, bf16[6,384,128]{2,1,0:T(8,128)(2,1)}, u32[]{:S(2)}) copy-start(bf16[6,384,128]{2,1,0:T(8,128)(2,1)} %param.12) | copy-start | bytes 1769476
  10.4 1.9 %copy-start.5 = (bf16[6,128,384]{2,1,0:T(8,128)(2,1)S(1)}, bf16[6,128,384]{2,1,0:T(8,128)(2,1)}, u32[]{:S(2)}) copy-start(bf16[6,128,384]{2,1,0:T(8,128)(2,1)} %param.10) | copy-start | bytes 1769476
  15.9 0.8 copy-start.2
  17.0 7.1 %copy-start.1 = (s32[32]{0:T(128)S(1)}, s32[32]{0:T(128)}, u32[]{:S(2)}) copy-start(s32[32]{0:T(128)} %param.17) | copy-start | bytes 388
  18.8 11.3 %all-to-all-start = ((bf16[8,2,5760]{2,1,0:T(2,128)(2,1)}), bf16[8,2,5760]{2,1,0:T(2,128)(2,1)S(1)}, u32[]{:S(2)}, u32[]{:S(2)}) async-start(bf16[8,2,5760]{2,1,0:T(2,128)(2,1)} %reshape.324), calls=%async_computation | async-start | bytes 368640 | tf_op jit(solution)/shard_map/all_to_all | solution.py:65
  24.0 29.3 %reduce-scatter.2.cloned.1.call-start = ((), (), s32[]{:S(2)}) async-start(), calls=%async_computation.5 | async-start | bytes 655360 | tf_op jit(solution)/shard_map/reduce_scatter | solution.py:69
  30.8 1.4 %copy-start.6 = (f32[128]{0:T(128)S(1)}, f32[128]{0:T(128)}, u32[]{:S(2)}) copy-start(f32[128]{0:T(128)} %param.14) | copy-start | bytes 1540
  30.8 22.4 %copy-start.3 = (f32[120]{0:T(128)S(1)}, f32[120]{0:T(128)}, u32[]{:S(2)}) copy-start(f32[120]{0:T(128)} %param.13) | copy-start | bytes 1444
  56.0 9.0 %all-to-all-start.1 = ((bf16[4,2,3840]{2,1,0:T(2,128)(2,1)}), bf16[4,2,3840]{2,1,0:T(2,128)(2,1)S(1)}, u32[]{:S(2)}, u32[]{:S(2)}) async-start(bf16[4,2,3840]{2,1,0:T(2,128)(2,1)} %reshape.326), calls=%async_computation.2 | async-start | bytes 122880 | tf_op jit(solution)/shard_map/all_to_all | solution.py:96
  82.7 9.7 %all-to-all-start.3 = ((bf16[8,2,5760]{2,1,0:T(2,128)(2,1)}), bf16[8,2,5760]{2,1,0:T(2,128)(2,1)S(1)}, u32[]{:S(2)}, u32[]{:S(2)}) async-start(bf16[8,2,5760]{2,1,0:T(2,128)(2,1)} %reshape.330), calls=%async_computation.4 | async-start | bytes 368640 | tf_op jit(solution)/shard_map/all_to_all | solution.py:100
Sparse Core Ops, SparseCore 0:
  32.2 20.9 reduce-scatter.1

commit v2 on v1

--- a/solution.py
+++ b/solution.py
@@ -1,9 +1,17 @@
+import functools
 import math
 
 import jax
 import jax.numpy as jnp
 from jax import lax
+from jax.experimental import pallas as pl
+from jax.experimental.pallas import tpu as pltpu
 from jax.sharding import PartitionSpec as P
+
+MESH = pl.DeviceIdType.MESH
+PART = 3
+GELU_A = math.sqrt(2.0 / math.pi)
+GELU_B = 0.044715 * GELU_A
 
 
 def column_layers(column_rows, weight_in, bias_in, weight_out):
@@ -108,11 +116,334 @@
     updated = (columns.astype(jnp.float32) + tendency.astype(jnp.float32)).astype(jnp.bfloat16)
     return (updated, spectral)
 
+def spread(blocks, width):
+    blocks = list(blocks)
+    group = lax.broadcasted_iota(jnp.int32, blocks[0].shape, 1) // width
+    lanes = blocks[0].shape[1]
+    step = 1
+    while step < len(blocks):
+        upper = (group & step) != 0
+        for i in range(len(blocks)):
+            if i & step == 0:
+                low, high = blocks[i], blocks[i + step]
+                blocks[i] = jnp.where(upper, pltpu.roll(high, step * width, 1), low)
+                blocks[i + step] = jnp.where(
+                    upper, high, pltpu.roll(low, lanes - step * width, 1)
+                )
+        step *= 2
+    return blocks
+
+
+def fused_kernel(
+    lat_count,
+    lon_count,
+    lat_rows,
+    lon_cols,
+    grid_ref,
+    w_in_ref,
+    bias_ref,
+    w_out_ref,
+    quad_ref,
+    diff_ref,
+    leg_ref,
+    chan_ref,
+    wave_ref,
+    out_ref,
+    spec_ref,
+    cols_ref,
+    rows_ref,
+    send1,
+    recv1,
+    send2,
+    recv2,
+    send_sem1,
+    recv_sem1,
+    send_sem2,
+    recv_sem2,
+):
+    f32, bf16, i32 = jnp.float32, jnp.bfloat16, jnp.int32
+    iota = lambda shape, dim: lax.broadcasted_iota(i32, shape, dim)
+    channels = grid_ref.shape[1]
+    layers = w_in_ref.shape[0]
+    slots, lat_total, top = leg_ref.shape
+    waves = wave_ref.shape[1]
+    per_dev = channels // lat_count
+    devices = lat_count * lon_count
+    pad = send1.shape[1]
+    wide = send1.shape[2]
+    trig_rows = 2 * waves
+    lon_total = lon_cols * lon_count
+    my_lat, my_lon = lax.axis_index("lat"), lax.axis_index("lon")
+    me = my_lat * lon_count + my_lon
+
+    barrier = pltpu.get_barrier_semaphore()
+
+    def peer(i):
+        other = lax.rem(me + i, devices)
+        return other, {"lat": other // lon_count, "lon": lax.rem(other, lon_count)}
+
+    @pl.loop(1, devices)
+    def _(i):
+        pl.semaphore_signal(barrier, inc=1, device_id=peer(i)[1], device_id_type=MESH)
+
+    def column_of(row, size):
+        eye = iota((size, size), 0) == iota((size, size), 1)
+        return jnp.sum(jnp.where(eye, row, jnp.zeros_like(row)), 1, keepdims=True)
+
+    chan_row = chan_ref[...]
+    chosen = iota((channels, channels), 0) == chan_row
+    order = jnp.where(chosen, 1.0, 0.0).astype(bf16)
+    unorder = jnp.where(iota((channels, channels), 1) == column_of(chan_row, channels), 1.0, 0.0)
+    unorder = unorder.astype(bf16)
+
+    wave_f = wave_ref[...].astype(f32)
+    wave_col = column_of(wave_f, waves)
+
+    def slot_of(row):
+        inner = row & (2 * slots - 1)
+        return (row // (2 * slots)) * slots + (inner & (slots - 1)), inner // slots
+
+    def trig(wave, part, place):
+        angle = wave * place
+        angle = angle + part * (lon_total / 4.0)
+        angle = angle - lon_total * jnp.floor((angle + 0.5) * (1.0 / lon_total))
+        return jnp.cos(angle * (2.0 * math.pi / lon_total)) * (1.0 / math.sqrt(lon_total))
+
+    slot_a, part_a = slot_of(iota((trig_rows, 1), 0))
+    wave_a = jnp.sum(jnp.where(iota((trig_rows, waves), 1) == slot_a, wave_f, 0.0), 1, keepdims=True)
+    lon_a = (iota((trig_rows, lon_cols), 1) + my_lon * lon_cols).astype(f32)
+    trig_in = trig(wave_a, part_a.astype(f32), lon_a).astype(bf16)
+    slot_b, part_b = slot_of(iota((1, trig_rows), 1))
+    wave_b = jnp.sum(jnp.where(iota((waves, trig_rows), 0) == slot_b, wave_col, 0.0), 0, keepdims=True)
+    lon_b = (iota((lon_cols, trig_rows), 0) + my_lon * lon_cols).astype(f32)
+    trig_out = trig(wave_b, part_b.astype(f32), lon_b).astype(bf16)
+
+    rows_ref[...] = jnp.zeros_like(rows_ref)
+
+    part_rows = PART * lon_cols
+
+    def column_part(p, carry):
+        start = pl.multiple_of(p * part_rows, part_rows)
+        x = grid_ref[pl.ds(start, part_rows), :].astype(f32)
+        for layer in range(layers):
+            inv = lax.rsqrt(jnp.mean(x * x, axis=-1, keepdims=True) + 1e-06)
+            normed = (x * inv).astype(bf16)
+            pre = jnp.dot(normed, w_in_ref[layer], preferred_element_type=f32)
+            pre = pre + bias_ref[pl.ds(layer, 1), :]
+            inner = pre * (GELU_A + GELU_B * (pre * pre))
+            half = 0.5 * pre
+            act = (half + half * jnp.tanh(inner)).astype(bf16)
+            x = x + jnp.dot(act, w_out_ref[layer], preferred_element_type=f32)
+        cols = x.astype(bf16)
+        cols_ref[pl.ds(start, part_rows), :] = cols
+        ordered = jnp.dot(cols, order, preferred_element_type=f32).astype(bf16)
+        for q in range(PART):
+            partial = jnp.dot(
+                trig_in, ordered[q * lon_cols : (q + 1) * lon_cols], preferred_element_type=f32
+            )
+            rows_ref[pl.ds(p * PART + q, trig_rows, stride=pad), :] = partial
+        return carry
+
+    lax.fori_loop(0, lat_rows // PART, column_part, 0)
+
+    for b in range(lon_count):
+        for r in range(2):
+            first = (b * 2 + r) * slots
+            got = spread(
+                [rows_ref[(first + s) * pad : (first + s + 1) * pad, :] for s in range(slots)], per_dev
+            )
+            for a in range(lat_count):
+                send1[a * lon_count + b, :, r * channels : (r + 1) * channels] = got[a].astype(bf16)
+
+    pl.semaphore_wait(barrier, devices - 1)
+
+    def exchange(send, recv, send_sem, recv_sem, chunk_of):
+        def copy(i):
+            other, place = peer(i)
+            return pltpu.make_async_remote_copy(
+                src_ref=send.at[chunk_of(other)],
+                dst_ref=recv.at[me],
+                send_sem=send_sem.at[other],
+                recv_sem=recv_sem.at[me],
+                device_id=place,
+                device_id_type=MESH,
+            )
+
+        @pl.loop(1, devices)
+        def _(i):
+            copy(i).start()
+
+        recv[me] = send[chunk_of(me)]
+
+        def finish():
+            @pl.loop(1, devices)
+            def _(i):
+                other, place = peer(i)
+                pltpu.make_async_remote_copy(
+                    src_ref=send.at[chunk_of(other)],
+                    dst_ref=recv.at[other],
+                    send_sem=send_sem.at[other],
+                    recv_sem=recv_sem.at[other],
+                    device_id=place,
+                    device_id_type=MESH,
+                ).wait()
+
+        return finish
+
+    finish = exchange(send1, recv1, send_sem1, recv_sem1, lambda other: other)
+
+    lat_pad = lat_count * pad
+    spect = slots * top
+    inner_row = iota((lat_pad, lat_total), 0)
+    lat_of = jnp.where(
+        (inner_row & (pad - 1)) < lat_rows, (inner_row // pad) * lat_rows + (inner_row & (pad - 1)), -1
+    )
+    chosen_lat = lat_of == iota((lat_pad, lat_total), 1)
+    quad_col = jnp.sum(jnp.where(chosen_lat, quad_ref[...], 0.0), 1, keepdims=True)
+    place_lat = jnp.where(chosen_lat, 1.0, 0.0).astype(bf16)
+    leg = jnp.zeros((lat_pad, spect), f32)
+    for s in range(slots):
+        rows = jnp.dot(place_lat, leg_ref[s], preferred_element_type=f32).astype(bf16)
+        into = iota((top, spect), 1) == iota((top, spect), 0) + s * top
+        leg = leg + jnp.dot(rows, jnp.where(into, 1.0, 0.0).astype(bf16), preferred_element_type=f32)
+    leg_t = jnp.transpose(leg).astype(bf16)
+    leg = leg.astype(bf16)
+
+    diff_col = column_of(diff_ref[...], channels)
+    diff_row = jnp.sum(jnp.where(chosen, diff_col, 0.0), 0, keepdims=True)
+    diff_sorted = column_of(diff_row, channels)
+    lane = iota((channels, wide), 1)
+    mine = iota((channels, wide), 0) == (lane & (per_dev - 1)) + my_lat * per_dev
+    diff_lane = jnp.sum(jnp.where(mine, diff_sorted, 0.0), 0, keepdims=True)
+    row_n = iota((spect, 1), 0)
+    degree = (row_n & (top - 1)).astype(f32)
+    damping = diff_lane * (degree * (degree + 1.0)) / float(top * top)
+    slot_n = row_n // top
+    wave_n = jnp.sum(
+        jnp.where(iota((spect, waves), 1) == slot_n + my_lon * slots, wave_f, 0.0), 1, keepdims=True
+    )
+    lane_slot = (iota((spect, wide), 1) & (channels - 1)) // per_dev
+    kept = (lane_slot == slot_n) & (degree >= wave_n)
+    scale = 1.0 / (1.0 + damping)
+
+    finish()
+    fourier = jnp.zeros((lat_pad, wide), f32)
+    for b in range(lon_count):
+        for_lon = jnp.concatenate([recv1[a * lon_count + b] for a in range(lat_count)], 0)
+        fourier = fourier + for_lon.astype(f32)
+    weighted = (fourier * quad_col).astype(bf16)
+    raw = jnp.dot(leg_t, weighted, preferred_element_type=f32)
+    spectral = jnp.where(kept, raw * scale, 0.0)
+    back = jnp.dot(leg, spectral.astype(bf16), preferred_element_type=f32).astype(bf16)
+    for a in range(lat_count):
+        send2[a] = back[a * pad : (a + 1) * pad]
+    finish = exchange(send2, recv2, send_sem2, recv_sem2, lambda other: other // lon_count)
+    folded = spectral[:top]
+    for s in range(1, slots):
+        folded = folded + spectral[s * top : (s + 1) * top]
+    spec_ref[...] = folded
+    finish()
+
+    for b in range(lon_count):
+        for r in range(2):
+            first = (b * 2 + r) * slots
+            got = spread(
+                [
+                    recv2[a * lon_count + b, :, r * channels : (r + 1) * channels].astype(f32)
+                    for a in range(lat_count)
+                ],
+                per_dev,
+            )
+            whole = jnp.concatenate(got, 0).astype(bf16)
+            rows_ref[first * pad : (first + slots) * pad, :] = jnp.dot(
+                whole, unorder, preferred_element_type=f32
+            )
+    for l in range(lat_rows):
+        coeffs = rows_ref[pl.ds(l, trig_rows, stride=pad), :].astype(bf16)
+        tendency = jnp.dot(trig_out, coeffs, preferred_element_type=f32).astype(bf16)
+        here = slice(l * lon_cols, (l + 1) * lon_cols)
+        out_ref[here, :] = (cols_ref[here, :].astype(f32) + tendency.astype(f32)).astype(bf16)
+
+
+def fused(
+    grid_state,
+    weight_in,
+    bias_in,
+    weight_out,
+    quad_weights,
+    diffusion,
+    legendre,
+    chan_table,
+    wave_table,
+):
+    lat_rows, lon_cols, channels = grid_state.shape
+    lat_count = lax.axis_size("lat")
+    lon_count = lax.axis_size("lon")
+    slots, _, top = legendre.shape
+    waves = wave_table.shape[0]
+    devices = lat_count * lon_count
+    pad = 16
+    wide = 2 * channels
+    vmem = pl.BlockSpec(memory_space=pltpu.VMEM)
+    updated, spec = pl.pallas_call(
+        functools.partial(fused_kernel, lat_count, lon_count, lat_rows, lon_cols),
+        out_shape=(
+            jax.ShapeDtypeStruct((lat_rows * lon_cols, channels), jnp.bfloat16),
+            jax.ShapeDtypeStruct((top, wide), jnp.float32),
+        ),
+        in_specs=[vmem] * 9,
+        out_specs=(vmem, vmem),
+        scratch_shapes=[
+            pltpu.VMEM((lat_rows * lon_cols, channels), jnp.bfloat16),
+            pltpu.VMEM((2 * waves * pad, channels), jnp.float32),
+            pltpu.VMEM((devices, pad, wide), jnp.bfloat16),
+            pltpu.VMEM((devices, pad, wide), jnp.bfloat16),
+            pltpu.VMEM((lat_count, pad, wide), jnp.bfloat16),
+            pltpu.VMEM((devices, pad, wide), jnp.bfloat16),
+            pltpu.SemaphoreType.DMA((devices,)),
+            pltpu.SemaphoreType.DMA((devices,)),
+            pltpu.SemaphoreType.DMA((devices,)),
+            pltpu.SemaphoreType.DMA((devices,)),
+        ],
+        compiler_params=pltpu.CompilerParams(
+            collective_id=0, has_side_effects=True, vmem_limit_bytes=40 * 2**20
+        ),
+    )(
+        grid_state.reshape(lat_rows * lon_cols, channels),
+        weight_in,
+        bias_in,
+        weight_out,
+        quad_weights[None, :],
+        diffusion[None, :],
+        legendre,
+        chan_table[None, :],
+        wave_table[None, :],
+    )
+    spectral = spec.reshape(top, 2, slots, channels // lat_count).transpose(2, 3, 1, 0)
+    return updated.reshape(lat_rows, lon_cols, channels), spectral
+
+
+def by_size(*arrays):
+    grid_state, legendre, wave_table = arrays[0], arrays[6], arrays[8]
+    lat_rows, lon_cols, channels = grid_state.shape
+    slots, _, top = legendre.shape
+    fits = (
+        channels == 128
+        and slots == lax.axis_size("lat")
+        and slots & (slots - 1) == 0
+        and top & (top - 1) == 0
+        and slots * lax.axis_size("lon") == wave_table.shape[0]
+        and lat_rows <= 16
+        and lat_rows % PART == 0
+        and lon_cols % 16 == 0
+    )
+    return (fused if fits else local)(*arrays)
+
 
 def solution(mesh):
     placed = (P("lat", "lon", None), P(), P(), P(), P(), P(), P("lon", None, None), P(), P())
     return jax.shard_map(
-        local,
+        by_size,
         mesh=mesh,
         in_specs=placed,
         out_specs=(P("lat", "lon", None), P("lon", "lat", None, None)),

time: 101 us -> 40.6 us (0.40)
  waiting for transfers between devices: 37.4 us -> 0 us
  Pallas kernels: 0 us -> 34.8 us
  between operations: 14.3 us -> 0.75 us
  starting transfers between devices: 12.1 us -> 0 us
  local copies, waits for them, and re-layouts: 14.7 us -> 4.78 us
  matrix products: 9.23 us -> 0 us
  blocking collectives: 9.13 us -> 0 us
  other arithmetic: 3.88 us -> 0 us
    pallas_call x0 -> x1, Pallas kernels: none -> 34.8 us  [fused(): pl.pallas_call(functools.partial(fused_kernel, lat_count, lon_count, lat_...]
    reduce_scatter x1 -> x0, waiting for transfers between devices: 20.7 us -> none  [local(): lax.psum_scatter(jnp.einsum('srj,ljk->skrl', trig_rows, levels, preferred...]
    all_to_all x3 -> x0, waiting for transfers between devices: 16.7 us -> none  [the longest x1 5.87 us: local(): lax.all_to_all(ordered, 'lat', split_axis=2, concat_axis=0, tiled=True)]
    all_to_all x3 -> x0, starting transfers between devices: 12 us -> none  [the longest x1 5.18 us: local(): lax.all_to_all(ordered, 'lat', split_axis=2, concat_axis=0, tiled=True)]
    dot_general x12 -> x0, matrix products: 9.23 us -> none  [the longest x6 6.23 us: column_layers(): jnp.dot(activation, weight_out[layer_idx], preferred_element_type=jnp.flo...]
    all_to_all x1 -> x0, blocking collectives: 9.13 us -> none  [local(): lax.all_to_all(band_tendency, 'lon', split_axis=1, concat_axis=0, tiled=T...]
    unnamed x23 -> x19, local copies, waits for them, and re-layouts: 9.62 us -> 4.68 us
    all_to_all x5 -> x0, local copies, waits for them, and re-layouts: 2.41 us -> none  [the longest x2 1.38 us: local(): lax.all_to_all(band_tendency, 'lon', split_axis=1, concat_axis=0, tiled=T...]
  transfers between devices with their start and end apart: 4 -> 0, of which waited for: 4 -> 0; matrix products, arithmetic and copies ran while one was open for 2% -> 0% of each run, Pallas kernels for 0% -> 0%
where the time goes in v2:
time: 40.6 us; the launch traced here: 40.4 us
  Pallas kernels  34.8 us (86%)
  local copies, waits for them, and re-layouts  4.78 us (12%)
  between operations  0.75 us (2%)
    pallas_call x1, Pallas kernels, fused(): pl.pallas_call(functools.partial(fused_kernel, lat_count, lon_count, lat_...  34.8 us
    unnamed x19, local copies, waits for them, and re-layouts  4.68 us

profile of v2, /device:TPU:0, one launch (start us, length us, event | category | flops | bytes accessed | tf_op | source)
XLA Modules:
  0.0 40.4 jit_solution(8465168960141836587)
XLA Ops:
  0.6 0.0 copy-start.2
  0.6 0.0 copy-start.3
  0.7 0.0 copy-start.4
  0.7 0.0 copy-start.5
  0.7 0.0 copy-start.6
  0.7 0.0 copy-start.7
  0.7 1.1 %copy.13.leg_ref = bf16[8,120,32]{2,1,0:T(8,128)(2,1)S(1)} copy(bf16[8,120,32]{1,2,0:T(8,128)(2,1)} %param.15) | data formatting | bytes 122880 | tf_op args[6]
  1.8 0.0 copy-done.2
  1.8 0.0 copy-done.3
  1.8 0.0 copy-done.4
  1.8 0.0 copy-done.5
  1.8 0.0 copy-done.6
  1.8 0.0 copy-done.7
  1.9 0.0 copy-start
  1.9 1.1 %copy-done = bf16[6,128,384]{2,1,0:T(8,128)(2,1)S(1)} copy-done((bf16[6,128,384]{2,1,0:T(8,128)(2,1)S(1)}, bf16[6,128,384]{2,1,0:T(8,128)(2,1)}, u32[]{:S(2)}) %copy-start) | copy-done | bytes 589848
  2.9 0.0 copy-start.1
  2.9 1.1 %copy-done.1 = bf16[6,384,128]{2,1,0:T(8,128)(2,1)S(1)} copy-done((bf16[6,384,128]{2,1,0:T(8,128)(2,1)S(1)}, bf16[6,384,128]{2,1,0:T(8,128)(2,1)}, u32[]{:S(2)}) %copy-start.1) | copy-done | bytes 589848
  4.0 34.8 %shard_map.104 = (bf16[720,128]{1,0:T(8,128)(2,1)S(1)}, f32[32,256]{1,0:T(8,128)S(1)}) custom-call(bf16[720,128]{1,0:T(8,128)(2,1)S(1)} %bitcast.9, bf16[6,128,384]{2,1,0:T(8,128)(2,1)S(1)} %copy-done, f32[6,384]{1,0:T(8,128)S(1)} %copy-done.3, bf16[6,384,128]{2,1,0:T(8,128)(2,1)S(1)} %copy-done.1, f32[1,120]{1,0:T(1,128)S(1)} %bitcast.11, ...), custom_call_target="tpu_custom_call" | custom-call | tf_op jit(solution)/shard_map/pallas_call | solution.py:388
  38.8 0.1 copy.14
  38.9 0.8 %copy.15 = f32[8,16,2,32]{3,2,1,0:T(2,128)} copy(f32[8,16,2,32]{3,1,0,2:T(8,128)S(1)} %bitcast.15) | data formatting | bytes 65536
  39.7 0.7 %copy.17 = bf16[15,48,128]{2,1,0:T(8,128)(2,1)} copy(bf16[15,48,128]{2,1,0:T(8,128)(2,1)S(1)} %bitcast.10) | data formatting | bytes 368640
Async XLA Ops:
  0.6 1.2 %copy-start.2 = (bf16[15,48,128]{2,1,0:T(8,128)(2,1)S(1)}, bf16[15,48,128]{2,1,0:T(8,128)(2,1)}, u32[]{:S(2)}) copy-start(bf16[15,48,128]{2,1,0:T(8,128)(2,1)} %param.9) | copy-start | bytes 552964
  0.6 1.2 %copy-start.3 = (f32[6,384]{1,0:T(8,128)S(1)}, f32[6,384]{1,0:T(8,128)}, u32[]{:S(2)}) copy-start(f32[6,384]{1,0:T(8,128)} %bias_ref.1) | copy-start | bytes 27652
  0.7 1.2 %copy-start.4 = (f32[120]{0:T(128)S(1)}, f32[120]{0:T(128)}, u32[]{:S(2)}) copy-start(f32[120]{0:T(128)} %param.13) | copy-start | bytes 1444
  0.7 1.2 %copy-start.5 = (f32[128]{0:T(128)S(1)}, f32[128]{0:T(128)}, u32[]{:S(2)}) copy-start(f32[128]{0:T(128)} %param.14) | copy-start | bytes 1540
  0.7 1.2 %copy-start.6 = (s32[128]{0:T(128)S(1)}, s32[128]{0:T(128)}, u32[]{:S(2)}) copy-start(s32[128]{0:T(128)} %param.16) | copy-start | bytes 1540
  0.7 1.2 %copy-start.7 = (s32[32]{0:T(128)S(1)}, s32[32]{0:T(128)}, u32[]{:S(2)}) copy-start(s32[32]{0:T(128)} %param.17) | copy-start | bytes 388
  1.9 1.1 %copy-start = (bf16[6,128,384]{2,1,0:T(8,128)(2,1)S(1)}, bf16[6,128,384]{2,1,0:T(8,128)(2,1)}, u32[]{:S(2)}) copy-start(bf16[6,128,384]{2,1,0:T(8,128)(2,1)} %w_in_ref.1) | copy-start | bytes 1769476
  2.9 1.1 %copy-start.1 = (bf16[6,384,128]{2,1,0:T(8,128)(2,1)S(1)}, bf16[6,384,128]{2,1,0:T(8,128)(2,1)}, u32[]{:S(2)}) copy-start(bf16[6,384,128]{2,1,0:T(8,128)(2,1)} %w_out_ref.1) | copy-start | bytes 1769476

commit v3 on v2

--- a/solution.py
+++ b/solution.py
@@ -9,7 +9,7 @@
 from jax.sharding import PartitionSpec as P
 
 MESH = pl.DeviceIdType.MESH
-PART = 3
+WEIGHTS = pl.ANY
 GELU_A = math.sqrt(2.0 / math.pi)
 GELU_B = 0.044715 * GELU_A
 
@@ -139,10 +139,11 @@
     lon_count,
     lat_rows,
     lon_cols,
+    slots,
     grid_ref,
-    w_in_ref,
+    w_in_hbm,
     bias_ref,
-    w_out_ref,
+    w_out_hbm,
     quad_ref,
     diff_ref,
     leg_ref,
@@ -150,41 +151,95 @@
     wave_ref,
     out_ref,
     spec_ref,
+    w_in_ref,
+    w_out_ref,
     cols_ref,
     rows_ref,
+    legs,
     send1,
     recv1,
     send2,
     recv2,
-    send_sem1,
-    recv_sem1,
-    send_sem2,
-    recv_sem2,
+    low_ref,
+    recv3,
+    send4,
+    recv4,
+    w_sem,
+    leg_send,
+    leg_recv,
+    lat_send1,
+    lat_recv1,
+    lon_send2,
+    lon_recv2,
+    lon_send3,
+    lon_recv3,
+    lat_send4,
+    lat_recv4,
 ):
     f32, bf16, i32 = jnp.float32, jnp.bfloat16, jnp.int32
     iota = lambda shape, dim: lax.broadcasted_iota(i32, shape, dim)
     channels = grid_ref.shape[1]
     layers = w_in_ref.shape[0]
-    slots, lat_total, top = leg_ref.shape
+    spect, lat_total = leg_ref.shape
+    top = spect // slots
     waves = wave_ref.shape[1]
     per_dev = channels // lat_count
-    devices = lat_count * lon_count
-    pad = send1.shape[1]
-    wide = send1.shape[2]
+    wide = 2 * channels
     trig_rows = 2 * waves
     lon_total = lon_cols * lon_count
     my_lat, my_lon = lax.axis_index("lat"), lax.axis_index("lon")
-    me = my_lat * lon_count + my_lon
+
+    loads = []
+    for layer in range(layers):
+        into = pltpu.make_async_copy(w_in_hbm.at[layer], w_in_ref.at[layer], w_sem.at[0, layer])
+        out_of = pltpu.make_async_copy(w_out_hbm.at[layer], w_out_ref.at[layer], w_sem.at[1, layer])
+        into.start()
+        out_of.start()
+        loads.append((into, out_of))
 
     barrier = pltpu.get_barrier_semaphore()
 
-    def peer(i):
-        other = lax.rem(me + i, devices)
-        return other, {"lat": other // lon_count, "lon": lax.rem(other, lon_count)}
-
-    @pl.loop(1, devices)
-    def _(i):
-        pl.semaphore_signal(barrier, inc=1, device_id=peer(i)[1], device_id_type=MESH)
+    def lat_peer(i):
+        other = lax.rem(my_lat + i, lat_count)
+        return other, {"lat": other, "lon": my_lon}
+
+    def lon_peer(i):
+        other = lax.rem(my_lon + i, lon_count)
+        return other, {"lat": my_lat, "lon": other}
+
+    for i in range(1, lat_count):
+        pl.semaphore_signal(barrier, inc=1, device_id=lat_peer(i)[1], device_id_type=MESH)
+    for i in range(1, lon_count):
+        pl.semaphore_signal(barrier, inc=1, device_id=lon_peer(i)[1], device_id_type=MESH)
+
+    def exchange(peer_of, count, mine, source, target, send_sem, recv_sem):
+        waits = []
+        for i in range(1, count):
+            other, place = peer_of(i)
+            pltpu.make_async_remote_copy(
+                src_ref=source(other),
+                dst_ref=target(mine),
+                send_sem=send_sem(other),
+                recv_sem=recv_sem(mine),
+                device_id=place,
+                device_id_type=MESH,
+            ).start()
+            waits.append(
+                pltpu.make_async_remote_copy(
+                    src_ref=source(other),
+                    dst_ref=target(other),
+                    send_sem=send_sem(other),
+                    recv_sem=recv_sem(other),
+                    device_id=place,
+                    device_id_type=MESH,
+                )
+            )
+
+        def finish():
+            for w in waits:
+                w.wait()
+
+        return finish
 
     def column_of(row, size):
         eye = iota((size, size), 0) == iota((size, size), 1)
@@ -218,96 +273,93 @@
     lon_b = (iota((lon_cols, trig_rows), 0) + my_lon * lon_cols).astype(f32)
     trig_out = trig(wave_b, part_b.astype(f32), lon_b).astype(bf16)
 
-    rows_ref[...] = jnp.zeros_like(rows_ref)
-
-    part_rows = PART * lon_cols
-
-    def column_part(p, carry):
-        start = pl.multiple_of(p * part_rows, part_rows)
-        x = grid_ref[pl.ds(start, part_rows), :].astype(f32)
+    lat_pad = 16 * lat_count
+
+    def lat_of(place):
+        row = (place // (8 * lat_count)) * 8 + (place & 7)
+        device = (place // 8) & (lat_count - 1)
+        return jnp.where(row < lat_rows, device * lat_rows + row, -1)
+
+    by_row = lat_of(iota((lat_pad, lat_total), 0)) == iota((lat_pad, lat_total), 1)
+    quad_col = jnp.sum(jnp.where(by_row, quad_ref[...], 0.0), 1, keepdims=True)
+    lat_col = iota((lat_total, lat_pad), 0)
+    by_col = jnp.where(lat_of(iota((lat_total, lat_pad), 1)) == lat_col, 1.0, 0.0).astype(bf16)
+    legs[my_lon] = jnp.dot(leg_ref[...], by_col, preferred_element_type=f32).astype(bf16)
+
+    def column_part(low, high, first):
+        part = slice(low * lon_cols, high * lon_cols)
+        x = grid_ref[part, :].astype(f32)
         for layer in range(layers):
             inv = lax.rsqrt(jnp.mean(x * x, axis=-1, keepdims=True) + 1e-06)
             normed = (x * inv).astype(bf16)
+            if first:
+                loads[layer][0].wait()
             pre = jnp.dot(normed, w_in_ref[layer], preferred_element_type=f32)
             pre = pre + bias_ref[pl.ds(layer, 1), :]
             inner = pre * (GELU_A + GELU_B * (pre * pre))
             half = 0.5 * pre
             act = (half + half * jnp.tanh(inner)).astype(bf16)
+            if first:
+                loads[layer][1].wait()
             x = x + jnp.dot(act, w_out_ref[layer], preferred_element_type=f32)
         cols = x.astype(bf16)
-        cols_ref[pl.ds(start, part_rows), :] = cols
-        ordered = jnp.dot(cols, order, preferred_element_type=f32).astype(bf16)
-        for q in range(PART):
-            partial = jnp.dot(
-                trig_in, ordered[q * lon_cols : (q + 1) * lon_cols], preferred_element_type=f32
-            )
-            rows_ref[pl.ds(p * PART + q, trig_rows, stride=pad), :] = partial
-        return carry
-
-    lax.fori_loop(0, lat_rows // PART, column_part, 0)
-
-    for b in range(lon_count):
-        for r in range(2):
-            first = (b * 2 + r) * slots
-            got = spread(
-                [rows_ref[(first + s) * pad : (first + s + 1) * pad, :] for s in range(slots)], per_dev
-            )
+        cols_ref[part, :] = cols
+        return jnp.dot(cols, order, preferred_element_type=f32).astype(bf16)
+
+    def pack(h, low, high, ordered):
+        for l in range(low, low + 8):
+            if l < high:
+                q = (l - low) * lon_cols
+                partial = jnp.dot(trig_in, ordered[q : q + lon_cols], preferred_element_type=f32)
+            else:
+                partial = jnp.zeros((trig_rows, channels), f32)
+            rows_ref[h, pl.ds(l - low, trig_rows, stride=8), :] = partial
+        for b in range(lon_count):
+            got = []
+            for r in range(2):
+                first = (b * 2 + r) * slots
+                got.append(
+                    spread(
+                        [rows_ref[h, (first + s) * 8 : (first + s + 1) * 8, :] for s in range(slots)],
+                        per_dev,
+                    )
+                )
             for a in range(lat_count):
-                send1[a * lon_count + b, :, r * channels : (r + 1) * channels] = got[a].astype(bf16)
-
-    pl.semaphore_wait(barrier, devices - 1)
-
-    def exchange(send, recv, send_sem, recv_sem, chunk_of):
-        def copy(i):
-            other, place = peer(i)
-            return pltpu.make_async_remote_copy(
-                src_ref=send.at[chunk_of(other)],
-                dst_ref=recv.at[me],
-                send_sem=send_sem.at[other],
-                recv_sem=recv_sem.at[me],
-                device_id=place,
-                device_id_type=MESH,
-            )
-
-        @pl.loop(1, devices)
-        def _(i):
-            copy(i).start()
-
-        recv[me] = send[chunk_of(me)]
-
-        def finish():
-            @pl.loop(1, devices)
-            def _(i):
-                other, place = peer(i)
-                pltpu.make_async_remote_copy(
-                    src_ref=send.at[chunk_of(other)],
-                    dst_ref=recv.at[other],
-                    send_sem=send_sem.at[other],
-                    recv_sem=recv_sem.at[other],
-                    device_id=place,
-                    device_id_type=MESH,
-                ).wait()
-
+                send1[h, a, b] = jnp.concatenate([got[0][a], got[1][a]], 0).astype(bf16)
+
+    def lat_exchange(h, send, recv, send_sem, recv_sem):
+        finish = exchange(
+            lat_peer,
+            lat_count,
+            my_lat,
+            lambda other: send.at[h, other],
+            lambda other: recv.at[h, other],
+            lambda other: send_sem.at[h, other],
+            lambda other: recv_sem.at[h, other],
+        )
+        recv[h, my_lat] = send[h, my_lat]
         return finish
 
-    finish = exchange(send1, recv1, send_sem1, recv_sem1, lambda other: other)
-
-    lat_pad = lat_count * pad
-    spect = slots * top
-    inner_row = iota((lat_pad, lat_total), 0)
-    lat_of = jnp.where(
-        (inner_row & (pad - 1)) < lat_rows, (inner_row // pad) * lat_rows + (inner_row & (pad - 1)), -1
-    )
-    chosen_lat = lat_of == iota((lat_pad, lat_total), 1)
-    quad_col = jnp.sum(jnp.where(chosen_lat, quad_ref[...], 0.0), 1, keepdims=True)
-    place_lat = jnp.where(chosen_lat, 1.0, 0.0).astype(bf16)
-    leg = jnp.zeros((lat_pad, spect), f32)
-    for s in range(slots):
-        rows = jnp.dot(place_lat, leg_ref[s], preferred_element_type=f32).astype(bf16)
-        into = iota((top, spect), 1) == iota((top, spect), 0) + s * top
-        leg = leg + jnp.dot(rows, jnp.where(into, 1.0, 0.0).astype(bf16), preferred_element_type=f32)
-    leg_t = jnp.transpose(leg).astype(bf16)
-    leg = leg.astype(bf16)
+    def lon_exchange(source, recv, send_sem, recv_sem):
+        return exchange(
+            lon_peer,
+            lon_count,
+            my_lon,
+            source,
+            lambda other: recv.at[other],
+            lambda other: send_sem.at[other],
+            lambda other: recv_sem.at[other],
+        )
+
+    halves = ((0, min(8, lat_rows)), (8, lat_rows))
+    ordered = column_part(*halves[0], True)
+    pl.semaphore_wait(barrier, lat_count + lon_count - 2)
+    pack(0, *halves[0], ordered)
+    finish1 = [lat_exchange(0, send1, recv1, lat_send1, lat_recv1)]
+    finish_leg = lon_exchange(lambda other: legs.at[my_lon], legs, leg_send, leg_recv)
+    ordered = column_part(*halves[1], False)
+    pack(1, *halves[1], ordered)
+    finish1.append(lat_exchange(1, send1, recv1, lat_send1, lat_recv1))
 
     diff_col = column_of(diff_ref[...], channels)
     diff_row = jnp.sum(jnp.where(chosen, diff_col, 0.0), 0, keepdims=True)
@@ -315,54 +367,76 @@
     lane = iota((channels, wide), 1)
     mine = iota((channels, wide), 0) == (lane & (per_dev - 1)) + my_lat * per_dev
     diff_lane = jnp.sum(jnp.where(mine, diff_sorted, 0.0), 0, keepdims=True)
-    row_n = iota((spect, 1), 0)
-    degree = (row_n & (top - 1)).astype(f32)
+    degree = iota((top, wide), 0).astype(f32)
     damping = diff_lane * (degree * (degree + 1.0)) / float(top * top)
-    slot_n = row_n // top
-    wave_n = jnp.sum(
-        jnp.where(iota((spect, waves), 1) == slot_n + my_lon * slots, wave_f, 0.0), 1, keepdims=True
-    )
-    lane_slot = (iota((spect, wide), 1) & (channels - 1)) // per_dev
-    kept = (lane_slot == slot_n) & (degree >= wave_n)
+    slot_lane = (iota((waves, wide), 1) & (channels - 1)) // per_dev
+    wave_lane = jnp.sum(
+        jnp.where(iota((waves, wide), 0) == slot_lane + my_lon * slots, wave_col, 0.0), 0, keepdims=True
+    )
     scale = 1.0 / (1.0 + damping)
-
-    finish()
-    fourier = jnp.zeros((lat_pad, wide), f32)
+    lane_slot = (iota((top, wide), 1) & (channels - 1)) // per_dev
+
+    finish_leg()
+    leg_back = [jnp.transpose(legs[b].astype(f32)).astype(bf16) for b in range(lon_count)]
+    for finish in finish1:
+        finish()
     for b in range(lon_count):
-        for_lon = jnp.concatenate([recv1[a * lon_count + b] for a in range(lat_count)], 0)
-        fourier = fourier + for_lon.astype(f32)
-    weighted = (fourier * quad_col).astype(bf16)
-    raw = jnp.dot(leg_t, weighted, preferred_element_type=f32)
-    spectral = jnp.where(kept, raw * scale, 0.0)
-    back = jnp.dot(leg, spectral.astype(bf16), preferred_element_type=f32).astype(bf16)
-    for a in range(lat_count):
-        send2[a] = back[a * pad : (a + 1) * pad]
-    finish = exchange(send2, recv2, send_sem2, recv_sem2, lambda other: other // lon_count)
-    folded = spectral[:top]
-    for s in range(1, slots):
-        folded = folded + spectral[s * top : (s + 1) * top]
-    spec_ref[...] = folded
-    finish()
-
+        chunks = []
+        for h in range(2):
+            for a in range(lat_count):
+                chunk = recv1[h, a, b].astype(f32)
+                chunks.append(jnp.concatenate([chunk[:8], chunk[8:]], 1))
+        weighted = (jnp.concatenate(chunks, 0) * quad_col).astype(bf16)
+        raw = jnp.dot(legs[b], weighted, preferred_element_type=f32)
+        own = raw[:top]
+        for s in range(1, slots):
+            own = jnp.where(lane_slot == s, raw[s * top : (s + 1) * top], own)
+        send2[b] = own.astype(bf16)
+    finish2 = lon_exchange(lambda other: send2.at[other], recv2, lon_send2, lon_recv2)
+    recv2[my_lon] = send2[my_lon]
+    finish2()
+    raw = recv2[0].astype(f32)
+    for b in range(1, lon_count):
+        raw = raw + recv2[b].astype(f32)
+    spectral = jnp.where(degree >= wave_lane, raw * scale, 0.0)
+    low = spectral.astype(bf16)
+    low_ref[...] = low
+    finish3 = lon_exchange(lambda other: low_ref, recv3, lon_send3, lon_recv3)
+    recv3[my_lon] = low
+    spec_ref[...] = spectral
+    finish3()
+
+    blocks = []
     for b in range(lon_count):
-        for r in range(2):
-            first = (b * 2 + r) * slots
-            got = spread(
-                [
-                    recv2[a * lon_count + b, :, r * channels : (r + 1) * channels].astype(f32)
-                    for a in range(lat_count)
-                ],
-                per_dev,
-            )
-            whole = jnp.concatenate(got, 0).astype(bf16)
-            rows_ref[first * pad : (first + slots) * pad, :] = jnp.dot(
-                whole, unorder, preferred_element_type=f32
-            )
-    for l in range(lat_rows):
-        coeffs = rows_ref[pl.ds(l, trig_rows, stride=pad), :].astype(bf16)
-        tendency = jnp.dot(trig_out, coeffs, preferred_element_type=f32).astype(bf16)
-        here = slice(l * lon_cols, (l + 1) * lon_cols)
-        out_ref[here, :] = (cols_ref[here, :].astype(f32) + tendency.astype(f32)).astype(bf16)
+        coeffs = recv3[b].astype(f32)
+        blocks.append(
+            jnp.concatenate([jnp.where(lane_slot == s, coeffs, 0.0) for s in range(slots)], 0).astype(bf16)
+        )
+    finish4 = []
+    band = 8 * lat_count
+    for h in range(2):
+        for b in range(lon_count):
+            back = jnp.dot(leg_back[b][h * band : (h + 1) * band], blocks[b], preferred_element_type=f32)
+            for a in range(lat_count):
+                rows = back[a * 8 : (a + 1) * 8]
+                send4[h, a, b] = jnp.concatenate([rows[:, :channels], rows[:, channels:]], 0).astype(bf16)
+        finish4.append(lat_exchange(h, send4, recv4, lat_send4, lat_recv4))
+    for h in range(2):
+        finish4[h]()
+        for b in range(lon_count):
+            chunks = [recv4[h, a, b].astype(f32) for a in range(lat_count)]
+            for r in range(2):
+                first = (b * 2 + r) * slots
+                got = spread([c[r * 8 : (r + 1) * 8] for c in chunks], per_dev)
+                whole = jnp.concatenate(got, 0).astype(bf16)
+                rows_ref[h, first * 8 : (first + slots) * 8, :] = jnp.dot(
+                    whole, unorder, preferred_element_type=f32
+                )
+        for l in range(*halves[h]):
+            coeffs = rows_ref[h, pl.ds(l - 8 * h, trig_rows, stride=8), :].astype(bf16)
+            tendency = jnp.dot(trig_out, coeffs, preferred_element_type=f32).astype(bf16)
+            here = slice(l * lon_cols, (l + 1) * lon_cols)
+            out_ref[here, :] = (cols_ref[here, :].astype(f32) + tendency.astype(f32)).astype(bf16)
 
 
 def fused(
@@ -379,34 +453,52 @@
     lat_rows, lon_cols, channels = grid_state.shape
     lat_count = lax.axis_size("lat")
     lon_count = lax.axis_size("lon")
-    slots, _, top = legendre.shape
+    slots, lat_total, top = legendre.shape
     waves = wave_table.shape[0]
-    devices = lat_count * lon_count
-    pad = 16
     wide = 2 * channels
+    bf16 = jnp.bfloat16
     vmem = pl.BlockSpec(memory_space=pltpu.VMEM)
+    anywhere = pl.BlockSpec(memory_space=WEIGHTS)
+    chunks = pltpu.VMEM((2, lat_count, lon_count, 16, channels), bf16)
+    coeffs = pltpu.VMEM((lon_count, top, wide), bf16)
+    lat_sems = pltpu.SemaphoreType.DMA((2, lat_count))
+    lon_sems = pltpu.SemaphoreType.DMA((lon_count,))
     updated, spec = pl.pallas_call(
-        functools.partial(fused_kernel, lat_count, lon_count, lat_rows, lon_cols),
+        functools.partial(fused_kernel, lat_count, lon_count, lat_rows, lon_cols, slots),
         out_shape=(
-            jax.ShapeDtypeStruct((lat_rows * lon_cols, channels), jnp.bfloat16),
+            jax.ShapeDtypeStruct((lat_rows * lon_cols, channels), bf16),
             jax.ShapeDtypeStruct((top, wide), jnp.float32),
         ),
-        in_specs=[vmem] * 9,
+        in_specs=[vmem, anywhere, vmem, anywhere] + [vmem] * 5,
         out_specs=(vmem, vmem),
         scratch_shapes=[
-            pltpu.VMEM((lat_rows * lon_cols, channels), jnp.bfloat16),
-            pltpu.VMEM((2 * waves * pad, channels), jnp.float32),
-            pltpu.VMEM((devices, pad, wide), jnp.bfloat16),
-            pltpu.VMEM((devices, pad, wide), jnp.bfloat16),
-            pltpu.VMEM((lat_count, pad, wide), jnp.bfloat16),
-            pltpu.VMEM((devices, pad, wide), jnp.bfloat16),
-            pltpu.SemaphoreType.DMA((devices,)),
-            pltpu.SemaphoreType.DMA((devices,)),
-            pltpu.SemaphoreType.DMA((devices,)),
-            pltpu.SemaphoreType.DMA((devices,)),
+            pltpu.VMEM(weight_in.shape, bf16),
+            pltpu.VMEM(weight_out.shape, bf16),
+            pltpu.VMEM((lat_rows * lon_cols, channels), bf16),
+            pltpu.VMEM((2, 2 * waves * 8, channels), jnp.float32),
+            pltpu.VMEM((lon_count, slots * top, 16 * lat_count), bf16),
+            chunks,
+            chunks,
+            coeffs,
+            coeffs,
+            pltpu.VMEM((top, wide), bf16),
+            coeffs,
+            chunks,
+            chunks,
+            pltpu.SemaphoreType.DMA((2, weight_in.shape[0])),
+            lon_sems,
+            lon_sems,
+            lat_sems,
+            lat_sems,
+            lon_sems,
+            lon_sems,
+            lon_sems,
+            lon_sems,
+            lat_sems,
+            lat_sems,
         ],
         compiler_params=pltpu.CompilerParams(
-            collective_id=0, has_side_effects=True, vmem_limit_bytes=40 * 2**20
+            collective_id=0, has_side_effects=True, vmem_limit_bytes=60 * 2**20
         ),
     )(
         grid_state.reshape(lat_rows * lon_cols, channels),
@@ -415,7 +507,7 @@
         weight_out,
         quad_weights[None, :],
         diffusion[None, :],
-        legendre,
+        legendre.swapaxes(1, 2).reshape(slots * top, lat_total),
         chan_table[None, :],
         wave_table[None, :],
     )
@@ -433,8 +525,7 @@
         and slots & (slots - 1) == 0
         and top & (top - 1) == 0
         and slots * lax.axis_size("lon") == wave_table.shape[0]
-        and lat_rows <= 16
-        and lat_rows % PART == 0
+        and 8 < lat_rows <= 16
         and lon_cols % 16 == 0
     )
     return (fused if fits else local)(*arrays)

time: 40.6 us -> 34.7 us (0.85)
  Pallas kernels: 34.8 us -> 31.5 us
  local copies, waits for them, and re-layouts: 4.78 us -> 2.33 us
    pallas_call x1, Pallas kernels: 34.8 us -> 31.5 us  [fused(): pl.pallas_call(functools.partial(fused_kernel, lat_count, lon_count, lat_...]
    unnamed x19 -> x4, local copies, waits for them, and re-layouts: 4.68 us -> 1.44 us
    pallas_call x1, local copies, waits for them, and re-layouts: 0.1 us -> 0.89 us  [fused(): pl.pallas_call(functools.partial(fused_kernel, lat_count, lon_count, lat_...]
where the time goes in v3:
time: 34.7 us; the launch traced here: 34.5 us
  Pallas kernels  31.5 us (91%)
  local copies, waits for them, and re-layouts  2.33 us (7%)
  between operations  0.65 us (2%)
    pallas_call x1, Pallas kernels, fused(): pl.pallas_call(functools.partial(fused_kernel, lat_count, lon_count, lat_...  31.5 us
    unnamed x4, local copies, waits for them, and re-layouts  1.44 us
    pallas_call x1, local copies, waits for them, and re-layouts, fused(): pl.pallas_call(functools.partial(fused_kernel, lat_count, lon_count, lat_...  0.89 us

profile of v3, /device:TPU:0, one launch (start us, length us, event | category | flops | bytes accessed | tf_op | source)
XLA Modules:
  0.0 34.5 jit_solution(7233289294256801511)
XLA Ops:
  0.6 31.5 %shard_map.104 = (bf16[720,128]{1,0:T(8,128)(2,1)}, f32[32,256]{1,0:T(8,128)}) custom-call(bf16[720,128]{1,0:T(8,128)(2,1)} %bitcast.13, bf16[6,128,384]{2,1,0:T(8,128)(2,1)} %w_in_hbm.1, f32[6,384]{1,0:T(8,128)} %bias_ref.1, bf16[6,384,128]{2,1,0:T(8,128)(2,1)} %w_out_hbm.1, f32[1,120]{1,0:T(1,128)} %bitcast.16, f32[1,128]{1,0:T(1,128)} %bitcast.17, ...), custom_call_target="tpu_custom_call" | custom-call | tf_op jit(solution)/shard_map/pallas_call | solution.py:466
  32.2 0.0 copy-start
  32.2 0.9 %copy.12 = f32[32,256]{0,1:T(8,128)S(1)} copy(f32[32,256]{1,0:T(8,128)} %get-tuple-element.5) | data formatting | bytes 65536 | tf_op jit(solution)/shard_map/pallas_call | solution.py:466
  33.1 0.8 %copy.13 = f32[8,16,2,32]{3,2,1,0:T(2,128)} copy(f32[8,16,2,32]{3,1,0,2:T(8,128)S(1)} %bitcast.12) | data formatting | bytes 65536
  33.8 0.0 copy-done
  33.8 0.7 %copy.15 = bf16[15,48,128]{2,1,0:T(8,128)(2,1)} copy(bf16[15,48,128]{2,1,0:T(8,128)(2,1)S(1)} %bitcast.14) | data formatting | bytes 368640
Async XLA Ops:
  32.2 1.7 %copy-start = (bf16[720,128]{1,0:T(8,128)(2,1)S(1)}, bf16[720,128]{1,0:T(8,128)(2,1)}, u32[]{:S(2)}) copy-start(bf16[720,128]{1,0:T(8,128)(2,1)} %get-tuple-element.4) | copy-start | bytes 552964

commit v4 on v3

--- a/solution.py
+++ b/solution.py
@@ -10,6 +10,7 @@
 
 MESH = pl.DeviceIdType.MESH
 WEIGHTS = pl.ANY
+EARLY = 3
 GELU_A = math.sqrt(2.0 / math.pi)
 GELU_B = 0.044715 * GELU_A
 
@@ -212,6 +213,8 @@
     for i in range(1, lon_count):
         pl.semaphore_signal(barrier, inc=1, device_id=lon_peer(i)[1], device_id_type=MESH)
 
+    sent = []
+
     def exchange(peer_of, count, mine, source, target, send_sem, recv_sem):
         waits = []
         for i in range(1, count):
@@ -235,9 +238,11 @@
                 )
             )
 
+        sent.extend(waits)
+
         def finish():
             for w in waits:
-                w.wait()
+                w.wait_recv()
 
         return finish
 
@@ -285,6 +290,12 @@
     lat_col = iota((lat_total, lat_pad), 0)
     by_col = jnp.where(lat_of(iota((lat_total, lat_pad), 1)) == lat_col, 1.0, 0.0).astype(bf16)
     legs[my_lon] = jnp.dot(leg_ref[...], by_col, preferred_element_type=f32).astype(bf16)
+
+    finish_leg = []
+
+    def send_legendre():
+        pl.semaphore_wait(barrier, lat_count + lon_count - 2)
+        finish_leg.append(lon_exchange(lambda other: legs.at[my_lon], legs, leg_send, leg_recv))
 
     def column_part(low, high, first):
         part = slice(low * lon_cols, high * lon_cols)
@@ -302,6 +313,8 @@
             if first:
                 loads[layer][1].wait()
             x = x + jnp.dot(act, w_out_ref[layer], preferred_element_type=f32)
+            if first and layer == EARLY:
+                send_legendre()
         cols = x.astype(bf16)
         cols_ref[part, :] = cols
         return jnp.dot(cols, order, preferred_element_type=f32).astype(bf16)
@@ -353,10 +366,8 @@
 
     halves = ((0, min(8, lat_rows)), (8, lat_rows))
     ordered = column_part(*halves[0], True)
-    pl.semaphore_wait(barrier, lat_count + lon_count - 2)
     pack(0, *halves[0], ordered)
     finish1 = [lat_exchange(0, send1, recv1, lat_send1, lat_recv1)]
-    finish_leg = lon_exchange(lambda other: legs.at[my_lon], legs, leg_send, leg_recv)
     ordered = column_part(*halves[1], False)
     pack(1, *halves[1], ordered)
     finish1.append(lat_exchange(1, send1, recv1, lat_send1, lat_recv1))
@@ -376,7 +387,7 @@
     scale = 1.0 / (1.0 + damping)
     lane_slot = (iota((top, wide), 1) & (channels - 1)) // per_dev
 
-    finish_leg()
+    finish_leg[0]()
     leg_back = [jnp.transpose(legs[b].astype(f32)).astype(bf16) for b in range(lon_count)]
     for finish in finish1:
         finish()
@@ -403,7 +414,9 @@
     low_ref[...] = low
     finish3 = lon_exchange(lambda other: low_ref, recv3, lon_send3, lon_recv3)
     recv3[my_lon] = low
-    spec_ref[...] = spectral
+    by_channel = jnp.transpose(spectral)
+    for r in range(2):
+        spec_ref[:, r, :] = by_channel[r * channels : (r + 1) * channels]
     finish3()
 
     blocks = []
@@ -437,6 +450,8 @@
             tendency = jnp.dot(trig_out, coeffs, preferred_element_type=f32).astype(bf16)
             here = slice(l * lon_cols, (l + 1) * lon_cols)
             out_ref[here, :] = (cols_ref[here, :].astype(f32) + tendency.astype(f32)).astype(bf16)
+    for copy in sent:
+        copy.wait_send()
 
 
 def fused(
@@ -467,7 +482,7 @@
         functools.partial(fused_kernel, lat_count, lon_count, lat_rows, lon_cols, slots),
         out_shape=(
             jax.ShapeDtypeStruct((lat_rows * lon_cols, channels), bf16),
-            jax.ShapeDtypeStruct((top, wide), jnp.float32),
+            jax.ShapeDtypeStruct((channels, 2, top), jnp.float32),
         ),
         in_specs=[vmem, anywhere, vmem, anywhere] + [vmem] * 5,
         out_specs=(vmem, vmem),
@@ -511,7 +526,7 @@
         chan_table[None, :],
         wave_table[None, :],
     )
-    spectral = spec.reshape(top, 2, slots, channels // lat_count).transpose(2, 3, 1, 0)
+    spectral = spec.reshape(slots, channels // lat_count, 2, top)
     return updated.reshape(lat_rows, lon_cols, channels), spectral
 
 

time: 34.7 us -> 33 us (0.951)
  Pallas kernels: 31.5 us -> 29.9 us
    pallas_call x1, Pallas kernels: 31.5 us -> 29.9 us  [fused(): pl.pallas_call(functools.partial(fused_kernel, lat_count, lon_count, lat_...]
    pallas_call x1 -> x0, local copies, waits for them, and re-layouts: 0.89 us -> none  [fused(): pl.pallas_call(functools.partial(fused_kernel, lat_count, lon_count, lat_...]
    unnamed x4, local copies, waits for them, and re-layouts: 1.44 us -> 2.3 us
where the time goes in v4:
time: 33 us; the launch traced here: 32.8 us
  Pallas kernels  29.9 us (91%)
  local copies, waits for them, and re-layouts  2.3 us (7%)
  between operations  0.65 us (2%)
    pallas_call x1, Pallas kernels, fused(): pl.pallas_call(functools.partial(fused_kernel, lat_count, lon_count, lat_...  29.9 us
    unnamed x4, local copies, waits for them, and re-layouts  2.3 us

profile of v4, /device:TPU:0, one launch (start us, length us, event | category | flops | bytes accessed | tf_op | source)
XLA Modules:
  0.0 32.8 jit_solution(18289676037344413914)
XLA Ops:
  0.6 29.9 %shard_map.104 = (bf16[720,128]{1,0:T(8,128)(2,1)}, f32[128,2,32]{2,1,0:T(2,128)}) custom-call(bf16[720,128]{1,0:T(8,128)(2,1)} %bitcast.10, bf16[6,128,384]{2,1,0:T(8,128)(2,1)} %w_in_hbm.1, f32[6,384]{1,0:T(8,128)} %bias_ref.1, bf16[6,384,128]{2,1,0:T(8,128)(2,1)} %w_out_hbm.1, f32[1,120]{1,0:T(1,128)} %bitcast.14, f32[1,128]{1,0:T(1,128)} %bitcast.15, ...), custom_call_target="tpu_custom_call" | custom-call | tf_op jit(solution)/shard_map/pallas_call | solution.py:481
  30.5 0.0 copy-start
  30.5 1.6 %copy.13 = bf16[15,48,128]{2,1,0:T(8,128)(2,1)} copy(bf16[15,48,128]{2,1,0:T(8,128)(2,1)} %bitcast.11) | data formatting | bytes 368640
  32.2 0.0 copy-done
  32.2 0.7 %copy.14 = f32[8,16,2,32]{3,2,1,0:T(2,128)} copy(f32[8,16,2,32]{3,2,1,0:T(2,128)S(1)} %bitcast.12) | data formatting | bytes 65536
Async XLA Ops:
  30.5 1.7 %copy-start = (f32[128,2,32]{2,1,0:T(2,128)S(1)}, f32[128,2,32]{2,1,0:T(2,128)}, u32[]{:S(2)}) copy-start(f32[128,2,32]{2,1,0:T(2,128)} %get-tuple-element.5) | copy-start | bytes 98308
